TPU v7x, 32 devices: a whole 2x2x4 slice. The times are simulated.
32 devices in a mesh: dp: 8 (over z, y), tensor: 4 (over x, core).
Axes of the slice: x: 2, y: 2, z: 4, core: 2. Of those that a mesh axis runs over, the one named last changes fastest.
Arguments:
- hidden: bfloat16 [1024, 3072], P('dp', 'tensor'), may hold values from -6 to 6
- cotangent: bfloat16 [1024, 4096], P('dp', 'tensor'), may hold values from -6 to 6
- blocks: bfloat16 [256, 128, 128], P('tensor'), may hold values from -0.1875 to 0.1875
- block_pos: int32 [4, 64], P('tensor'), may hold values from 0 to 191, as said below
- owner_rank: int32 [4, 64], P('tensor'), may hold values from 0 to 63, each once within a row
- moment: float32 [4, 64, 128, 128], P('tensor', 'dp'), may hold values from -0.028125 to 0.028125
- second: float32 [4, 64, 128, 128], P('tensor', 'dp'), may hold values from 2.4414062e-06 to 3.90625e-05
Outputs:
- mixed: bfloat16 [1024, 4096], P('dp', 'tensor')
- hidden_grad: bfloat16 [1024, 3072], P('dp', 'tensor')
- new_moment: float32 [4, 64, 128, 128], P('tensor', 'dp')
- new_second: float32 [4, 64, 128, 128], P('tensor', 'dp')
- direction: float32 [4, 64, 128, 128], P('tensor', 'dp')
- new_blocks: bfloat16 [256, 128, 128], P('tensor')
Inputs may be any that keep to these rules, and one draw needn't show every extreme that they name: `block_pos`: each row holds 64 different positions of the 6 x 32 blocks of one slab, in no order. `owner_rank`: the block of rank k has its optimizer state at dp index k // 8.
All inputs are finite; a program needn't handle non-finite values.
Results may differ from a plain program's by a relative error of at most 0.017.
Values may be sent and summed in bfloat16 or wider, within the bound.
A program may use at most 64 MiB of HBM per device.

v0:
```python
import jax
import jax.numpy as jnp
from jax import lax
from jax.sharding import PartitionSpec as P


def shards(hidden, cotangent, blocks, block_pos, owner_rank, moment, second):
    token_count = hidden.shape[0]
    slot_count = blocks.shape[0]
    block_size = blocks.shape[1]
    row_blocks = hidden.shape[1] // block_size
    width = cotangent.shape[1] * lax.axis_size("tensor")
    col_blocks = width // block_size
    total_tokens = token_count * lax.axis_size("dp")
    owned = slot_count // lax.axis_size("dp")
    highest = lax.Precision.HIGHEST
    positions = block_pos[0]
    ranks = owner_rank[0]
    block_rows = positions // col_blocks
    block_cols = positions % col_blocks
    chosen_hid = jnp.take(hidden.reshape(token_count, row_blocks, block_size), block_rows, axis=1)
    col_hot = (block_cols[:, None] == jnp.arange(col_blocks)[None, :]).astype(jnp.float32)
    row_hot = (block_rows[:, None] == jnp.arange(row_blocks)[None, :]).astype(jnp.float32)
    contrib = jnp.einsum("nsa,sab->nsb", chosen_hid, blocks, preferred_element_type=jnp.float32)
    partial_value = jnp.einsum("nsb,sc->ncb", contrib, col_hot, precision=highest).reshape(
        token_count, width
    )
    mixed = lax.psum_scatter(
        partial_value.astype(jnp.bfloat16), "tensor", scatter_dimension=1, tiled=True
    )
    full_grad = lax.all_gather(cotangent, "tensor", axis=1, tiled=True)
    chosen_grad = jnp.take(
        full_grad.reshape(token_count, col_blocks, block_size), block_cols, axis=1
    )
    back = jnp.einsum("nsb,sab->nsa", chosen_grad, blocks, preferred_element_type=jnp.float32)
    hidden_grad = (
        jnp.einsum("nsa,sr->nra", back, row_hot, precision=highest)
        .reshape(token_count, row_blocks * block_size)
        .astype(jnp.bfloat16)
    )
    order = jnp.argsort(ranks)
    factor = 1.0 / total_tokens
    grads = (
        jnp.einsum("nsa,nsb->sab", chosen_hid, chosen_grad, preferred_element_type=jnp.float32)
        * factor
    )
    grads = jnp.take(grads, order, axis=0)
    mine = lax.psum_scatter(grads, "dp", scatter_dimension=0, tiled=True)
    owner_index = lax.axis_index("dp")
    mine_slots = lax.dynamic_slice_in_dim(order, owner_index * owned, owned)
    weights_own = jnp.take(blocks, mine_slots, axis=0).astype(jnp.float32)
    mom_next = 0.9 * moment[0] + 0.1 * mine
    sec_next = 0.999 * second[0] + 0.001 * mine * mine
    step_dir = mom_next / (jnp.sqrt(sec_next) + 1e-08)
    updated = (weights_own - 0.002 * (step_dir + 0.1 * weights_own)).astype(jnp.bfloat16)
    returned = lax.all_gather(updated, "dp", axis=0, tiled=True)
    new_blocks = jnp.take(returned, ranks, axis=0)
    return (mixed, hidden_grad, mom_next[None], sec_next[None], step_dir[None], new_blocks)


def solution(mesh):
    placed = (
        P("dp", "tensor"),
        P("dp", "tensor"),
        P("tensor", None, None),
        P("tensor", None),
        P("tensor", None),
        P("tensor", "dp", None, None),
        P("tensor", "dp", None, None),
    )
    return jax.shard_map(
        shards,
        mesh=mesh,
        in_specs=placed,
        out_specs=(
            P("dp", "tensor"),
            P("dp", "tensor"),
            P("tensor", "dp", None, None),
            P("tensor", "dp", None, None),
            P("tensor", "dp", None, None),
            P("tensor", None, None),
        ),
        check_vma=False,
    )
```

profile of v0, /device:TPU:0, one launch (start us, length us, event | category | flops | bytes accessed | tf_op | source)
XLA Modules:
  0.0 221.1 jit_solution(12170269456190844211)
XLA Ops:
  7.2 0.0 copy-start
  7.2 0.0 all-gather.3.cloned.1.call-start
  7.2 1.9 copy.31
  9.2 0.0 all-gather.3.cloned.1.call-update
  9.2 0.0 reduce-scatter.5.cloned.1.call-start
  9.2 1.1 copy.28
  10.3 0.2 copy.29
  10.5 0.7 fusion.30
  11.2 0.0 copy-start.4
  11.2 0.0 copy-start.3
  11.2 2.1 gather_fusion
  13.3 0.0 copy-done.4
  13.3 2.0 sort.17
  15.4 0.0 copy-done.3
  15.4 14.2 %all-gather.3.cloned.1.call-done = bf16[128,4096]{0,1:T(8,128)(2,1)} async-done(((bf16[128,1024]{0,1:T(8,128)(2,1)}), bf16[128,4096]{0,1:T(8,128)(2,1)}) %all-gather.3.cloned.1.call-update) | async-done | bytes 1048592 | tf_op jit(solution)/shard_map/all_gather | solution.py:31
  29.6 1.6 copy.32
  31.2 2.2 gather_fusion.1
  33.4 5.2 %convolution_multiply_fusion = f32[64,128,128]{2,1,0:T(8,128)} fusion(bf16[64,128,128]{2,1,0:T(8,128)(2,1)} %gather_fusion, pred[64]{0:T(512)(128)(4,1)S(1)} %get-tuple-element.38, bf16[64,128,128]{2,1,0:T(8,128)(2,1)} %gather_fusion.1, pred[64]{0:T(512)(128)(4,1)S(1)} %get-tuple-element.30), kind=kOutput, calls=%fused_computation.9 | convolution fusion | flops 271581184 | bytes 8388736 | tf_op jit(solution)/shard_map/nsa,nsb->sab/dot_general | solution.py:44
  38.6 5.0 %gather_fusion.2 = f32[64,128,128]{2,1,0:T(8,128)} fusion(f32[64,128,128]{2,1,0:T(8,128)} %convolution_multiply_fusion, s32[1024]{0:T(1024)S(1)} %pad_clamp_fusion.2), kind=kCustom, calls=%fused_computation.2 | custom fusion | bytes 8388864 | tf_op jit(solution)/shard_map/jit(_take)/gather | solution.py:47
  43.6 4.5 %broadcast_select_fusion = f32[64,128,128]{2,1,0:T(8,128)} fusion(f32[64,128,128]{2,1,0:T(8,128)} %gather_fusion.2, pred[64]{0:T(512)(128)(4,1)S(1)} %compare_and_fusion.2), kind=kLoop, calls=%fused_computation.16 | loop fusion | flops 1048576 | bytes 8388672 | tf_op jit(solution)/shard_map/jit(_take)/select_n | solution.py:47
  48.1 0.0 copy-start.1
  48.1 0.0 copy-start.2
  48.1 0.0 reduce-scatter.5.cloned.1.call-update
  48.1 0.0 all-gather.5.cloned.1.call-start
  48.2 0.1 compare_and_fusion
  48.2 0.0 copy-done
  48.3 0.6 gather_fusion.3
  48.9 87.3 %reduce-scatter.5.cloned.1.call-done = f32[8,128,128]{2,1,0:T(8,128)} async-done(((f32[64,128,128]{2,1,0:T(8,128)}), f32[8,128,128]{2,1,0:T(8,128)}) %reduce-scatter.5.cloned.1.call-update) | async-done | bytes 524304 | tf_op jit(solution)/shard_map/reduce_scatter | solution.py:48
  136.2 0.0 copy-done.1
  136.2 0.0 copy-done.2
  136.2 2.7 %fusion.19 = (bf16[8,128,128]{2,1,0:T(8,128)(2,1)}, f32[8,128,128]{2,1,0:T(8,128)}, f32[1,8,128,128]{3,2,1,0:T(8,128)}, f32[1,8,128,128]{3,2,1,0:T(8,128)}) fusion(bf16[8,128,128]{2,1,0:T(8,128)(2,1)S(1)} %gather_fusion.3, pred[8]{0:T(512)(128)(4,1)S(1)} %get-tuple-element.28, f32[8,128,128]{2,1,0:T(8,128)} %reduce-scatter.5.cloned.1.call-done, ...), kind=kLoop, calls=%fused_computation.29 | loop fusion | flops 2097152 | bytes 3670024 | tf_op jit(solution)/shard_map/convert_element_type | solution.py:55
  138.8 0.0 all-gather.5.cloned.1.call-update
  138.9 0.2 reduce-scatter.3.cloned.1.call-start
  139.1 2.4 %convolution_bitcast_fusion.1 = f32[128,64,128]{2,0,1:T(8,128)S(1)} fusion(bf16[64,128,128]{2,1,0:T(8,128)(2,1)S(1)} %copy-done, bf16[64,128,128]{2,1,0:T(8,128)(2,1)} %gather_fusion, pred[64]{0:T(512)(128)(4,1)S(1)} %get-tuple-element.38), kind=kOutput, calls=%fused_computation.11 | convolution fusion | flops 269484032 | bytes 8388672 | tf_op jit(solution)/shard_map/nsa,sab->nsb/dot_general | solution.py:24
  141.5 4.1 %fusion.8 = bf16[32,128,128]{2,0,1:T(8,128)(2,1)S(1)} fusion(f32[128,64,128]{2,0,1:T(8,128)S(1)} %convolution_bitcast_fusion.1, s32[64]{0:T(128)S(1)} %get-tuple-element.31), kind=kOutput, calls=%fused_computation.20 | convolution fusion | flops 403179520 | bytes 5243136 | tf_op jit(solution)/shard_map/nsb,sc->ncb/dot_general | solution.py:25
  145.5 1.4 copy.50
  146.9 0.0 reduce-scatter.3.cloned.1.call-update
  147.0 3.2 %convolution_bitcast_fusion = f32[128,64,128]{2,0,1:T(8,128)S(1)} fusion(bf16[64,128,128]{2,1,0:T(8,128)(2,1)S(1)} %copy-done, bf16[64,128,128]{2,1,0:T(8,128)(2,1)} %gather_fusion.1, pred[64]{0:T(512)(128)(4,1)S(1)} %get-tuple-element.30), kind=kOutput, calls=%fused_computation.10 | convolution fusion | flops 269484032 | bytes 8388672 | tf_op jit(solution)/shard_map/nsb,sab->nsa/dot_general | solution.py:35
  150.3 3.8 %fusion.14 = bf16[128,6,128]{2,1,0:T(8,128)(2,1)S(1)} fusion(f32[128,64,128]{2,0,1:T(8,128)S(1)} %convolution_bitcast_fusion, s32[64]{0:T(128)S(1)} %get-tuple-element.39), kind=kOutput, calls=%fused_computation.22 | convolution fusion | flops 75596160 | bytes 4391168 | tf_op jit(solution)/shard_map/nsa,sr->nra/dot_general | solution.py:37
  154.1 0.2 copy.34
  154.3 0.8 copy.36
  155.1 33.0 %all-gather.5.cloned.1.call-done = bf16[64,128,128]{2,1,0:T(8,128)(2,1)} async-done(((bf16[8,128,128]{2,1,0:T(8,128)(2,1)}), bf16[64,128,128]{2,1,0:T(8,128)(2,1)}) %all-gather.5.cloned.1.call-update) | async-done | bytes 2097168 | tf_op jit(solution)/shard_map/all_gather | solution.py:56
  188.1 3.7 %gather_fusion.4 = bf16[64,128,128]{2,1,0:T(8,128)(2,1)} fusion(bf16[64,128,128]{2,1,0:T(8,128)(2,1)} %all-gather.5.cloned.1.call-done, s32[1024]{0:T(1024)S(1)} %pad_clamp_fusion), kind=kCustom, calls=%fused_computation.4 | custom fusion | bytes 4194560 | tf_op jit(solution)/shard_map/jit(_take)/gather | solution.py:57
  191.8 3.2 %broadcast_select_fusion.3 = bf16[64,128,128]{2,1,0:T(8,128)(2,1)} fusion(bf16[64,128,128]{2,1,0:T(8,128)(2,1)} %gather_fusion.4, pred[64]{0:T(512)(128)(4,1)S(1)} %compare_and_fusion.1), kind=kLoop, calls=%fused_computation.19 | loop fusion | flops 1048576 | bytes 4194368 | tf_op jit(solution)/shard_map/jit(_take)/select_n | solution.py:57
  195.0 19.6 %reduce-scatter.3.cloned.1.call-done = bf16[128,1024]{1,0:T(8,128)(2,1)} async-done(((bf16[128,4096]{1,0:T(8,128)(2,1)}), bf16[128,1024]{1,0:T(8,128)(2,1)}) %reduce-scatter.3.cloned.1.call-update) | async-done | bytes 262160 | tf_op jit(solution)/shard_map/reduce_scatter | solution.py:28
  (10 shorter events, 0.1 us)
Async XLA Ops:
  7.2 41.1 %copy-start = (bf16[64,128,128]{2,1,0:T(8,128)(2,1)S(1)}, bf16[64,128,128]{2,1,0:T(8,128)(2,1)}, u32[]{:S(2)}) copy-start(bf16[64,128,128]{2,1,0:T(8,128)(2,1)} %param.9) | copy-start | bytes 6291460
  7.2 22.4 %all-gather.3.cloned.1.call-start = ((), (), s32[]{:S(2)}) async-start(), calls=%async_computation.3 | async-start | bytes 1310720 | tf_op jit(solution)/shard_map/all_gather | solution.py:31
  9.2 127.0 %reduce-scatter.5.cloned.1.call-start = ((), (), s32[]{:S(2)}) async-start(), calls=%async_computation.4 | async-start | bytes 4718592 | tf_op jit(solution)/shard_map/reduce_scatter | solution.py:48
  11.2 2.2 copy-start.4
  11.2 4.2 %copy-start.3 = (s32[1,64]{1,0:T(1,128)S(1)}, s32[1,64]{1,0:T(1,128)}, u32[]{:S(2)}) copy-start(s32[1,64]{1,0:T(1,128)} %param.10) | copy-start | bytes 772
  48.1 88.1 %copy-start.1 = (f32[1,8,128,128]{3,2,1,0:T(8,128)S(1)}, f32[1,8,128,128]{3,2,1,0:T(8,128)}, u32[]{:S(2)}) copy-start(f32[1,8,128,128]{3,2,1,0:T(8,128)} %param.13) | copy-start | bytes 1572868
  48.1 88.1 %copy-start.2 = (f32[1,8,128,128]{3,2,1,0:T(8,128)S(1)}, f32[1,8,128,128]{3,2,1,0:T(8,128)}, u32[]{:S(2)}) copy-start(f32[1,8,128,128]{3,2,1,0:T(8,128)} %param.12) | copy-start | bytes 1572868
  48.1 140.0 %all-gather.5.cloned.1.call-start = ((), (), s32[]{:S(2)}) async-start(), calls=%async_computation.5 | async-start | bytes 2359296 | tf_op jit(solution)/shard_map/all_gather | solution.py:56
  138.9 75.7 %reduce-scatter.3.cloned.1.call-start = ((), (), s32[]{:S(2)}) async-start(), calls=%async_computation.2 | async-start | bytes 1310720 | tf_op jit(solution)/shard_map/reduce_scatter | solution.py:28
Sparse Core Ops, SparseCore 0:
  10.2 19.4 all-gather.2
  48.2 87.8 reduce-scatter.4
  139.0 49.0 all-gather.4
  191.2 23.3 reduce-scatter.2
where the time goes:
time: 222 us; the launch traced here: 221 us
  waiting for transfers between devices  154 us (69%)
  local copies, waits for them, and re-layouts  20.9 us (9%)
  matrix products  18.6 us (8%)
  between operations  13.9 us (6%)
  other arithmetic  13.2 us (6%)
    reduce_scatter x1, waiting for transfers between devices, shards(): mine = lax.psum_scatter(grads, 'dp', scatter_dimension=0, tiled=True)  87.3 us
    all_gather x1, waiting for transfers between devices, shards(): returned = lax.all_gather(updated, 'dp', axis=0, tiled=True)  33 us
    reduce_scatter x1, waiting for transfers between devices, shards(): lax.psum_scatter(partial_value.astype(jnp.bfloat16), 'tensor', scatter_di...  19.6 us
    all_gather x1, waiting for transfers between devices, shards(): full_grad = lax.all_gather(cotangent, 'tensor', axis=1, tiled=True)  14.2 us
    unnamed x14, local copies, waits for them, and re-layouts  5.3 us
    dot_general x1, matrix products, shards(): jnp.einsum('nsa,nsb->sab', chosen_hid, chosen_grad, preferred_element_typ...  5.17 us
    gather x1, local copies, waits for them, and re-layouts, shards(): grads = jnp.take(grads, order, axis=0)  4.98 us
    select_n x2, other arithmetic, shards(): grads = jnp.take(grads, order, axis=0)  4.51 us
  transfers between devices with their start and end apart: 4, of which 4 were waited for; matrix products, arithmetic and copies ran while one was open for 13% of the time, Pallas kernels for 0%

commit v1 on v0

v1 whole, which is shorter than its diff:
```python
import functools

import jax
import jax.numpy as jnp
from jax import lax
from jax.experimental import pallas as pl
from jax.experimental.pallas import tpu as pltpu
from jax.sharding import PartitionSpec as P

CORES = 2
MESH = pl.DeviceIdType.MESH
F32 = jnp.float32
BF16 = jnp.bfloat16


def split_dp(dp):
    wide = 1
    while (wide * 2) ** 2 <= dp and dp % (wide * 2) == 0:
        wide *= 2
    return dp // wide, wide


def step_kernel(
    dims, hid, ct, blk, table, rank, mom, sec,
    mixed_o, hgrad_o, nm_o, ns_o, nd_o, nb_o,
    hid_all, hid_t, ct_all, ct_col, blk_v, dense, part_s, part_r, mixed_v, hgrad_v,
    grad_s, from_lo, from_hi, mom_v, sec_v, dir_v, gathered, listed,
    hid_r, ct_r, part_rs, lo_r, hi_r, ag_r,
    hid_ss, ct_ss, fwd_ss, core_ss, part_ss, rs_ss, agz_ss, agd_ss, agy_ss,
    loc, out_s,
):
    dp, tn = dims
    lines, wide = split_dp(dp)
    cores = CORES if tn % CORES == 0 else 1
    chips = tn // cores
    n, ff = hid.shape
    cw = ct.shape[1]
    width = cw * tn
    slots, bs = blk.shape[0], blk.shape[1]
    cols = width // bs
    row_blocks = ff // bs
    owned = mom.shape[0]
    chunks = grad_s.shape[1]
    cb = owned // chunks

    d = lax.axis_index("dp")
    t = lax.axis_index("tensor")
    z, y = d // wide, d % wide
    x, core = t // cores, t % cores

    def ys(i):
        return (y + i) % wide

    def xs(j):
        return ((x + j) % chips) * cores + core

    mate = x * cores + (core + 1) % cores

    barrier = pltpu.get_barrier_semaphore()
    for i in range(1, tn):
        pl.semaphore_signal(barrier, inc=1, device_id={"tensor": (t + i) % tn}, device_id_type=MESH)
    for i in range(1, wide):
        pl.semaphore_signal(barrier, inc=1, device_id={"dp": z * wide + ys(i)}, device_id_type=MESH)

    @pl.when(z > 0)
    def _():
        pl.semaphore_signal(barrier, inc=1, device_id={"dp": d - wide}, device_id_type=MESH)

    @pl.when(z < lines - 1)
    def _():
        pl.semaphore_signal(barrier, inc=1, device_id={"dp": d + wide}, device_id_type=MESH)

    my_rows = pl.ds(pl.multiple_of(y * n, n), n)
    my_cols = pl.ds(pl.multiple_of(t * cw, cw), cw)
    load_hid = pltpu.make_async_copy(hid, hid_all.at[my_rows, :], loc.at[0])
    load_ct = pltpu.make_async_copy(ct, ct_all.at[my_rows, my_cols], loc.at[1])
    load_blk = pltpu.make_async_copy(blk, blk_v.at[pl.ds(0, slots)], loc.at[2])
    load_mom = pltpu.make_async_copy(mom, mom_v, loc.at[3])
    load_sec = pltpu.make_async_copy(sec, sec_v, loc.at[4])
    for copy in (load_hid, load_blk, load_ct, load_mom, load_sec):
        copy.start()

    near = jnp.where(z > 0, 1, 0) + jnp.where(z < lines - 1, 1, 0)
    pl.semaphore_wait(barrier, tn - 1 + wide - 1 + near)

    def ct_slot(yy, tt):
        return ct_all.at[
            pl.ds(pl.multiple_of(yy * n, n), n), pl.ds(pl.multiple_of(tt * cw, cw), cw)
        ]

    def ct_copy(src, yy, tt, send, device):
        return pltpu.make_async_remote_copy(
            src_ref=src, dst_ref=ct_slot(yy, tt), send_sem=send,
            recv_sem=ct_r.at[yy * tn + tt], device_id=device, device_id_type=MESH,
        )

    def ct_arrival(yy, tt):
        ct_copy(ct_slot(yy, tt), yy, tt, ct_ss.at[0], {"tensor": mate}).wait_recv()

    sent = []

    def launch(copy):
        copy.start()
        sent.append(copy)

    for i in range(1, wide):
        launch(ct_copy(ct, y, t, ct_ss.at[i - 1], {"dp": z * wide + ys(i)}))
    for j in range(1, chips):
        launch(ct_copy(ct, y, t, ct_ss.at[wide - 1 + j - 1], {"tensor": xs(j)}))
    if cores > 1:
        launch(ct_copy(ct, y, t, ct_ss.at[wide + chips - 2], {"tensor": mate}))
    for i in range(1, wide):
        launch(pltpu.make_async_remote_copy(
            src_ref=hid, dst_ref=hid_all.at[my_rows, :], send_sem=hid_ss.at[i - 1],
            recv_sem=hid_r.at[y], device_id={"dp": z * wide + ys(i)}, device_id_type=MESH,
        ))

    blk_v[slots] = jnp.zeros((bs, bs), BF16)
    load_blk.wait()
    lanes = table.shape[1]

    def place(c, carry):
        for r in range(row_blocks):
            p = r * cols + c
            s = table[3 + p // lanes, p % lanes]
            dense[pl.ds(r * bs, bs), pl.ds(pl.multiple_of(c * bs, bs), bs)] = blk_v[s]
        return carry

    lax.fori_loop(0, cols, place, 0)
    load_hid.wait()
    tile = min(256, cw)

    def forward(k, carry):
        tt, c = k // (cw // tile), k % (cw // tile)
        value = jnp.dot(
            hid_all[my_rows, :],
            dense[:, pl.ds(pl.multiple_of(k * tile, tile), tile)],
            preferred_element_type=F32,
        )
        part_s[tt, :, pl.ds(pl.multiple_of(c * tile, tile), tile)] = value.astype(BF16)
        return carry

    lax.fori_loop(0, width // tile, forward, 0)

    load_ct.wait()
    for i in range(1, wide):
        yy = ys(i)
        ct_arrival(yy, t)
        for j in range(1, chips):
            launch(ct_copy(
                ct_slot(yy, t), yy, t, fwd_ss.at[(i - 1) * (chips - 1) + j - 1],
                {"tensor": xs(j)},
            ))
        if cores > 1:
            launch(ct_copy(ct_slot(yy, t), yy, t, core_ss.at[i - 1], {"tensor": mate}))
    for j in range(1, chips):
        ct_arrival(y, xs(j))
        if cores > 1:
            launch(ct_copy(
                ct_slot(y, xs(j)), y, xs(j), core_ss.at[wide - 1 + j - 1], {"tensor": mate}
            ))
    if cores > 1:
        for j in range(chips):
            ct_arrival(y, ((x + j) % chips) * cores + (core + 1) % cores)

    rtile = 256 if ff % 256 == 0 else bs

    def backward(k, carry):
        rows = pl.ds(pl.multiple_of(k * rtile, rtile), rtile)
        value = lax.dot_general(
            ct_all[my_rows, :], dense[rows, :], (((1,), (1,)), ((), ())),
            preferred_element_type=F32,
        )
        hgrad_v[:, rows] = value.astype(BF16)
        return carry

    lax.fori_loop(0, ff // rtile, backward, 0)
    store_hgrad = pltpu.make_async_copy(hgrad_v, hgrad_o, out_s.at[0])
    store_hgrad.start()

    for i in range(1, wide):
        yy = ys(i)
        pltpu.make_async_remote_copy(
            src_ref=hid, dst_ref=hid_all.at[pl.ds(pl.multiple_of(yy * n, n), n), :],
            send_sem=hid_ss.at[0], recv_sem=hid_r.at[yy],
            device_id={"tensor": mate}, device_id_type=MESH,
        ).wait_recv()

    def flip(k, carry):
        rows = pl.ds(pl.multiple_of(k * bs, bs), bs)
        hid_t[k] = hid_all[:, rows].T
        return carry

    lax.fori_loop(0, row_blocks, flip, 0)

    for i in range(1, wide):
        for j in range(1, chips):
            yy = ys(i)
            ct_arrival(yy, xs(j))
            if cores > 1:
                launch(ct_copy(
                    ct_slot(yy, xs(j)), yy, xs(j),
                    core_ss.at[wide + chips - 2 + (i - 1) * (chips - 1) + j - 1],
                    {"tensor": mate},
                ))
    if cores > 1:
        for i in range(1, wide):
            for j in range(chips):
                ct_arrival(ys(i), ((x + j) % chips) * cores + (core + 1) % cores)

    def by_column(k, carry):
        ct_col[k] = ct_all[:, pl.ds(pl.multiple_of(k * bs, bs), bs)]
        return carry

    lax.fori_loop(0, cols, by_column, 0)

    for i in range(1, tn):
        peer = (t + i) % tn
        launch(pltpu.make_async_remote_copy(
            src_ref=part_s.at[peer], dst_ref=part_r.at[t], send_sem=part_ss.at[i - 1],
            recv_sem=part_rs.at[t], device_id={"tensor": peer}, device_id_type=MESH,
        ))

    def own_grad(owner, c, k):
        r = (owner * wide + y) * owned + c * cb + k
        return jnp.dot(hid_t[table[1, r]], ct_col[table[2, r]], preferred_element_type=F32)

    def sum_copy(owner, c, up):
        into, sems = (from_lo, lo_r) if up else (from_hi, hi_r)
        return pltpu.make_async_remote_copy(
            src_ref=grad_s.at[owner, c], dst_ref=into.at[owner, c],
            send_sem=rs_ss.at[owner * chunks + c], recv_sem=sems.at[owner * chunks + c],
            device_id={"dp": d + wide if up else d - wide}, device_id_type=MESH,
        )

    def pass_sum(owner, c, up):
        inner = (z > 0) if up else (z < lines - 1)
        into = from_lo if up else from_hi

        @pl.when(inner)
        def _():
            sum_copy(owner, c, up).wait_recv()
            for k in range(cb):
                value = own_grad(owner, c, k) + into[owner, c, k].astype(F32)
                grad_s[owner, c, k] = value.astype(BF16)

        @pl.when(jnp.logical_not(inner))
        def _():
            for k in range(cb):
                grad_s[owner, c, k] = own_grad(owner, c, k).astype(BF16)

        sum_copy(owner, c, up).start()

    def pass_sums(c):
        for dist in range(lines - 1, 0, -1):
            @pl.when(z + dist < lines)
            def _():
                pass_sum(z + dist, c, True)

            @pl.when(z - dist >= 0)
            def _():
                pass_sum(z - dist, c, False)

    def new_copy(owner, yy, c, send, device):
        slot = gathered.at[pl.ds((owner * wide + yy) * owned + c * cb, cb)]
        return pltpu.make_async_remote_copy(
            src_ref=slot, dst_ref=slot, send_sem=send,
            recv_sem=ag_r.at[(owner * wide + yy) * chunks + c],
            device_id=device, device_id_type=MESH,
        )

    def new_up(owner, c):
        return new_copy(owner, y, c, agz_ss.at[owner * chunks + c], {"dp": d + wide})

    def new_down(owner, c):
        sem = agd_ss.at[owner * chunks + c]
        return new_copy(owner, y, c, sem, {"dp": d - wide})

    def new_side(owner, c, i):
        sem = agy_ss.at[(owner * chunks + c) * (wide - 1) + i - 1]
        return new_copy(owner, y, c, sem, {"dp": z * wide + ys(i)})

    factor = 1.0 / (n * dp)

    def finish(c):
        for low in (True, False):
            @pl.when((z > 0) if low else (z < lines - 1))
            def _():
                sum_copy(z, c, low).wait_recv()
        lo_on = jnp.where(z > 0, 1, 0)
        hi_on = jnp.where(z < lines - 1, 1, 0)
        for k in range(cb):
            at = c * cb + k
            dir_v[at] = own_grad(z, c, k)

            @pl.when(lo_on == 1)
            def _():
                dir_v[at] += from_lo[z, c, k].astype(F32)

            @pl.when(hi_on == 1)
            def _():
                dir_v[at] += from_hi[z, c, k].astype(F32)

            g = dir_v[at] * factor
            m = 0.9 * mom_v[at] + 0.1 * g
            v = 0.999 * sec_v[at] + 0.001 * g * g
            step = m / (jnp.sqrt(v) + 1e-08)
            mom_v[at] = m
            sec_v[at] = v
            dir_v[at] = step
            w = blk_v[table[0, d * owned + at]].astype(F32)
            gathered[d * owned + at] = (w - 0.002 * (step + 0.1 * w)).astype(BF16)

        @pl.when(z < lines - 1)
        def _():
            new_up(z, c).start()

        @pl.when(z > 0)
        def _():
            new_down(z, c).start()

        for i in range(1, wide):
            new_side(z, c, i).start()

    def pass_new(c):
        for dist in range(1, lines):
            @pl.when(z - dist >= 0)
            def _():
                new_up(z - dist, c).wait_recv()

                @pl.when(z < lines - 1)
                def _():
                    new_up(z - dist, c).start()

                for i in range(1, wide):
                    new_side(z - dist, c, i).start()

            @pl.when(z + dist < lines)
            def _():
                new_down(z + dist, c).wait_recv()

                @pl.when(z > 0)
                def _():
                    new_down(z + dist, c).start()

                for i in range(1, wide):
                    new_side(z + dist, c, i).start()

    load_mom.wait()
    load_sec.wait()
    pass_sums(0)
    for c in range(chunks):
        finish(c)
        if c + 1 < chunks:
            pass_sums(c + 1)
        if c > 0:
            pass_new(c - 1)
    store_nm = pltpu.make_async_copy(mom_v, nm_o, out_s.at[1])
    store_ns = pltpu.make_async_copy(sec_v, ns_o, out_s.at[2])
    store_nd = pltpu.make_async_copy(dir_v, nd_o, out_s.at[3])
    for copy in (store_nm, store_ns, store_nd):
        copy.start()

    for i in range(1, tn):
        peer = (t + i) % tn
        pltpu.make_async_remote_copy(
            src_ref=part_s.at[peer], dst_ref=part_r.at[peer], send_sem=part_ss.at[i - 1],
            recv_sem=part_rs.at[peer], device_id={"tensor": peer}, device_id_type=MESH,
        ).wait_recv()

    def add_parts(k, carry):
        at = pl.ds(pl.multiple_of(k * bs, bs), bs)
        value = part_s[t, :, at].astype(F32)
        for i in range(1, tn):
            value = value + part_r[(t + i) % tn, :, at].astype(F32)
        mixed_v[:, at] = value.astype(BF16)
        return carry

    lax.fori_loop(0, cw // bs, add_parts, 0)
    store_mixed = pltpu.make_async_copy(mixed_v, mixed_o, out_s.at[4])
    store_mixed.start()

    pass_new(chunks - 1)
    for c in range(chunks):
        for owner in range(lines):
            for i in range(1, wide):
                new_copy(owner, ys(i), c, agy_ss.at[0], {"tensor": mate}).wait_recv()

    def relist(s, carry):
        listed[s] = gathered[rank[0, s]]
        return carry

    lax.fori_loop(0, slots, relist, 0, unroll=8)
    store_nb = pltpu.make_async_copy(listed, nb_o, out_s.at[5])
    store_nb.start()

    for copy in sent:
        copy.wait_send()
    for c in range(chunks):
        for owner in range(lines):
            @pl.when(owner != z)
            def _():
                sum_copy(owner, c, True).wait_send()

            @pl.when((owner <= z) & (z < lines - 1))
            def _():
                new_up(owner, c).wait_send()

            @pl.when((owner >= z) & (z > 0))
            def _():
                new_down(owner, c).wait_send()

            for i in range(1, wide):
                new_side(owner, c, i).wait_send()
    for copy in (store_hgrad, store_nm, store_ns, store_nd, store_mixed, store_nb):
        copy.wait()


def tables(pos, rank, row_blocks, cols):
    slots = pos.shape[0]
    lanes = max(128, -(-slots // 128) * 128)
    rows = -(-(3 + -(-row_blocks * cols // lanes)) // 8) * 8
    flat = jnp.arange(rows * lanes, dtype=jnp.int32)[:, None]
    part = flat // lanes
    slot = jnp.arange(slots, dtype=jnp.int32)[None, :]
    pos, rank = pos[None, :], rank[None, :]
    key = jnp.where(part < 3, rank + part * lanes, pos + 3 * lanes)
    by_rank = jnp.where(part == 0, slot, jnp.where(part == 1, pos // cols, pos % cols))
    value = jnp.where(part < 3, by_rank, slot - slots)
    found = jnp.sum(jnp.where(key == flat, value, 0), axis=1, dtype=jnp.int32)
    return jnp.where(part[:, 0] < 3, found, found + slots).reshape(rows, lanes)


def shards(dims, hidden, cotangent, blocks, block_pos, owner_rank, moment, second):
    dp, tn = dims
    lines, wide = split_dp(dp)
    chips = max(tn // CORES, 1)
    n, ff = hidden.shape
    cw = cotangent.shape[1]
    width = cw * tn
    slots, bs, _ = blocks.shape
    owned = moment.shape[1]
    chunks = 2 if owned % 2 == 0 else 1
    cb = owned // chunks
    table = tables(block_pos[0], owner_rank[0], ff // bs, width // bs)
    own_shape = moment.shape[1:]
    any_spec = pl.BlockSpec(memory_space=pl.ANY)
    smem_spec = pl.BlockSpec(memory_space=pltpu.SMEM)
    dma = pltpu.SemaphoreType.DMA

    def some(count):
        return dma((max(count, 1),))

    flops = 2 * n * width * ff * 2 + 2 * n * wide * slots * bs * bs
    out = pl.pallas_call(
        functools.partial(step_kernel, dims),
        out_shape=(
            jax.ShapeDtypeStruct((n, cw), BF16),
            jax.ShapeDtypeStruct((n, ff), BF16),
            jax.ShapeDtypeStruct(own_shape, F32),
            jax.ShapeDtypeStruct(own_shape, F32),
            jax.ShapeDtypeStruct(own_shape, F32),
            jax.ShapeDtypeStruct(blocks.shape, BF16),
        ),
        in_specs=[any_spec, any_spec, any_spec, smem_spec, smem_spec, any_spec, any_spec],
        out_specs=(any_spec,) * 6,
        scratch_shapes=[
            pltpu.VMEM((wide * n, ff), BF16),
            pltpu.VMEM((ff // bs, bs, wide * n), BF16),
            pltpu.VMEM((wide * n, width), BF16),
            pltpu.VMEM((width // bs, wide * n, bs), BF16),
            pltpu.VMEM((slots + 1, bs, bs), BF16),
            pltpu.VMEM((ff, width), BF16),
            pltpu.VMEM((tn, n, cw), BF16),
            pltpu.VMEM((tn, n, cw), BF16),
            pltpu.VMEM((n, cw), BF16),
            pltpu.VMEM((n, ff), BF16),
            pltpu.VMEM((lines, chunks, cb, bs, bs), BF16),
            pltpu.VMEM((lines, chunks, cb, bs, bs), BF16),
            pltpu.VMEM((lines, chunks, cb, bs, bs), BF16),
            pltpu.VMEM(own_shape, F32),
            pltpu.VMEM(own_shape, F32),
            pltpu.VMEM(own_shape, F32),
            pltpu.VMEM((slots, bs, bs), BF16),
            pltpu.VMEM((slots, bs, bs), BF16),
            some(wide),
            some(wide * tn),
            some(tn),
            some(lines * chunks),
            some(lines * chunks),
            some(dp * chunks),
            some(wide - 1),
            some(wide + chips - 1),
            some((wide - 1) * (chips - 1)),
            some(wide + chips - 2 + (wide - 1) * (chips - 1)),
            some(tn - 1),
            some(lines * chunks),
            some(lines * chunks),
            some(lines * chunks),
            some(lines * chunks * (wide - 1)),
            dma((6,)),
            dma((6,)),
        ],
        compiler_params=pltpu.CompilerParams(
            collective_id=0, has_side_effects=True, vmem_limit_bytes=56 * 1024 * 1024
        ),
        cost_estimate=pl.CostEstimate(
            flops=flops, bytes_accessed=16 * 1024 * 1024, transcendentals=0
        ),
        name="train_step",
    )(hidden, cotangent, blocks, table, owner_rank, moment[0], second[0])
    mixed, hidden_grad, new_moment, new_second, direction, new_blocks = out
    return (
        mixed, hidden_grad, new_moment[None], new_second[None], direction[None], new_blocks
    )


def solution(mesh):
    placed = (
        P("dp", "tensor"),
        P("dp", "tensor"),
        P("tensor", None, None),
        P("tensor", None),
        P("tensor", None),
        P("tensor", "dp", None, None),
        P("tensor", "dp", None, None),
    )
    return jax.shard_map(
        functools.partial(shards, (mesh.shape["dp"], mesh.shape["tensor"])),
        mesh=mesh,
        in_specs=placed,
        out_specs=(
            P("dp", "tensor"),
            P("dp", "tensor"),
            P("tensor", "dp", None, None),
            P("tensor", "dp", None, None),
            P("tensor", "dp", None, None),
            P("tensor", None, None),
        ),
        check_vma=False,
    )
```

time: 222 us -> 90.7 us (0.41)
  waiting for transfers between devices: 154 us -> 0 us
  Pallas kernels: 0 us -> 78.2 us
  matrix products: 18.6 us -> 0 us
  between operations: 13.9 us -> 0.69 us
  local copies, waits for them, and re-layouts: 20.9 us -> 9.3 us
  other arithmetic: 13.2 us -> 2.14 us
    reduce_scatter x2 -> x0, waiting for transfers between devices: 107 us -> none  [the longest x1 87.3 us: shards(): mine = lax.psum_scatter(grads, 'dp', scatter_dimension=0, tiled=True)]
    pallas_call x0 -> x1, Pallas kernels: none -> 78.2 us  [shards(): pl.pallas_call(functools.partial(step_kernel, dims), out_shape=(jax.Shape...]
    all_gather x2 -> x0, waiting for transfers between devices: 47.1 us -> none  [the longest x1 33 us: shards(): returned = lax.all_gather(updated, 'dp', axis=0, tiled=True)]
    dot_general x5 -> x0, matrix products: 18.6 us -> none  [the longest x1 5.17 us: shards(): jnp.einsum('nsa,nsb->sab', chosen_hid, chosen_grad, preferred_element_typ...]
    gather x5 -> x0, local copies, waits for them, and re-layouts: 13.6 us -> none  [the longest x1 4.98 us: shards(): grads = jnp.take(grads, order, axis=0)]
    select_n x5 -> x1, other arithmetic: 8.35 us -> 0.61 us  [tables(): return jnp.where(part[:, 0] < 3, found, found + slots).reshape(rows, lanes)]
    unnamed x14 -> x10, local copies, waits for them, and re-layouts: 5.3 us -> 9.3 us
    convert_element_type x1 -> x0, other arithmetic: 2.67 us -> none  [shards(): (weights_own - 0.002 * (step_dir + 0.1 * weights_own)).astype(jnp.bfloat16)]
  transfers between devices with their start and end apart: 4 -> 0, of which waited for: 4 -> 0; matrix products, arithmetic and copies ran while one was open for 13% -> 0% of each run, Pallas kernels for 0% -> 0%
where the time goes in v1:
time: 90.7 us; the launch traced here: 90.4 us
  Pallas kernels  78.2 us (86%)
  local copies, waits for them, and re-layouts  9.3 us (10%)
  other arithmetic  2.14 us (2%)
    pallas_call x1, Pallas kernels, shards(): pl.pallas_call(functools.partial(step_kernel, dims), out_shape=(jax.Shape...  78.2 us
    unnamed x10, local copies, waits for them, and re-layouts  9.3 us

profile of v1, /device:TPU:0, one launch (start us, length us, event | category | flops | bytes accessed | tf_op | source)
XLA Modules:
  0.0 90.4 jit_solution(3381570355504025313)
XLA Ops:
  0.7 0.7 add_bitcast_fusion
  1.3 0.8 select_reduce_fusion
  2.2 0.6 add_select_fusion.table
  2.8 78.2 %train_step.1 = (bf16[128,1024]{1,0:T(8,128)(2,1)}, bf16[128,768]{1,0:T(8,128)(2,1)}, f32[8,128,128]{2,1,0:T(8,128)}, f32[8,128,128]{2,1,0:T(8,128)}, f32[8,128,...) custom-call(bf16[128,768]{1,0:T(8,128)(2,1)} %hid.1, bf16[128,1024]{1,0:T(8,128)(2,1)} %ct.1, bf16[64,128,128]{2,1,0:T(8,128)(2,1)} %blk.1, ...), custom_call_target="tpu_custom_call" | custom-call | flops 2147483648 | bytes 16777216 | tf_op jit(solution)/shard_map/train_step/pallas_call | solution.py:455
  81.0 0.0 copy-start.1
  81.1 0.0 copy-start
  81.1 1.8 %copy.19 = bf16[128,1024]{1,0:T(8,128)(2,1)} copy(bf16[128,1024]{1,0:T(8,128)(2,1)} %get-tuple-element.29) | data formatting | bytes 524288
  82.9 1.6 %copy.20 = bf16[128,768]{1,0:T(8,128)(2,1)} copy(bf16[128,768]{1,0:T(8,128)(2,1)} %get-tuple-element.30) | data formatting | bytes 393216
  84.5 1.9 %copy.21 = f32[1,8,128,128]{3,2,1,0:T(8,128)} copy(f32[1,8,128,128]{3,2,1,0:T(8,128)} %bitcast.16) | data formatting | bytes 1048576
  86.4 1.9 %copy.22 = f32[1,8,128,128]{3,2,1,0:T(8,128)} copy(f32[1,8,128,128]{3,2,1,0:T(8,128)} %bitcast.15) | data formatting | bytes 1048576
  88.2 0.0 copy-done.1
  88.2 0.8 copy.23
  89.0 0.0 copy-done
  89.0 1.3 %copy.24 = bf16[64,128,128]{2,1,0:T(8,128)(2,1)} copy(bf16[64,128,128]{2,1,0:T(8,128)(2,1)S(1)} %copy-done) | data formatting | bytes 4194304
  (4 shorter events, 0.0 us)
Async XLA Ops:
  81.0 7.2 %copy-start.1 = (f32[8,128,128]{2,1,0:T(8,128)S(1)}, f32[8,128,128]{2,1,0:T(8,128)}, u32[]{:S(2)}) copy-start(f32[8,128,128]{2,1,0:T(8,128)} %get-tuple-element.16) | copy-start | bytes 1572868
  81.1 8.0 %copy-start = (bf16[64,128,128]{2,1,0:T(8,128)(2,1)S(1)}, bf16[64,128,128]{2,1,0:T(8,128)(2,1)}, u32[]{:S(2)}) copy-start(bf16[64,128,128]{2,1,0:T(8,128)(2,1)} %get-tuple-element.34) | copy-start | bytes 6291460
